TPU v7x, 256 devices: a whole 4x4x8 slice. The times are simulated.
256 devices in a mesh: gx: 32 (over y, x, core), gy: 8 (over z).
Axes of the slice: x: 4, y: 4, z: 8, core: 2. Of those that a mesh axis runs over, the one named last changes fastest.
Arguments:
- wave_coeffs: bfloat16 [1536, 131072], P('gy', 'gx'), may hold values from -6 to 6
- projectors: bfloat16 [1024, 131072], P(None, 'gx'), may hold values from -0.03125 to 0.03125
- miller_index: int32 [3, 131072], P(None, 'gx'), may hold values from -32 to 31, as said below
- occupations: float32 [1536], P('gy'), may hold values from 0 to 2
- species_map: int32 [128], replicated, may hold values from 0 to 3
- proj_counts: int32 [128], replicated, may hold values from 1 to 8, as said below
- onsite_base: float32 [4, 8, 8], replicated, may hold values from -5 to 5
Outputs:
- new_bands: float32 [1536, 131072], P('gy', 'gx')
Inputs may be any that keep to these rules, and one draw needn't show every extreme that they name: `miller_index`: each column is a distinct lattice vector; columns run through whole shells of equal squared length in increasing order, the last shell possibly in part. `proj_counts`: some atom has exactly 8 projectors and some atom exactly one.
All inputs are finite; a program needn't handle non-finite values.
Results may differ from a plain program's by a relative error of at most 0.0031.
Values may be sent and summed in bfloat16 or wider, within the bound.
A program may use at most 64 MiB of HBM per device.

v0:
```python
import jax
import jax.numpy as jnp
from jax import lax
from jax.sharding import PartitionSpec as P

PMAX = 8
ITERS = 2


kinetic_unit = 1.0 / 600.0
hubbard_weight = 2.0
step_length = 0.5


def kinetic_of(miller_index):
    components = miller_index.astype(jnp.float32)
    metric = jnp.array([1.5, 1.0, 0.5], dtype=jnp.float32)
    return jnp.sum(metric[:, None] * components * components, axis=0) * kinetic_unit


def teter_factor(kinetic, band_kinetic):
    scaled_kinetic = kinetic[None, :] / band_kinetic[:, None]
    numerator = 27.0 + scaled_kinetic * (18.0 + scaled_kinetic * (12.0 + 8.0 * scaled_kinetic))
    return numerator / (numerator + 16.0 * scaled_kinetic**4)


def live_table(counts, slot_width):
    slot_index = jnp.arange(slot_width, dtype=jnp.int32)
    return (slot_index[None, :] < counts[:, None]).astype(jnp.float32)


def finish_onsite(masked, density, live_slots, species_rows, onsite_base):
    atom_count, slot_width, band_here = masked.shape
    kind_count = onsite_base.shape[0]
    onehot = (species_rows[:, None] == jnp.arange(kind_count, dtype=jnp.int32)[None, :]).astype(
        jnp.float32
    )
    symmetric = 0.5 * (onsite_base + jnp.swapaxes(onsite_base, 1, 2))
    base_here = jnp.dot(
        onehot,
        symmetric.reshape(kind_count, slot_width * slot_width),
        precision=lax.Precision.HIGHEST,
    ).reshape(atom_count, slot_width, slot_width)
    onsite = base_here + hubbard_weight * density
    return (
        jnp.einsum("apq,aqb->apb", onsite, masked, precision=lax.Precision.HIGHEST)
        * live_slots[:, :, None]
    )


def local(
    wave_coeffs, projectors, miller_index, occupations, species_map, proj_counts, onsite_base
):
    kinetic = kinetic_of(miller_index)
    band_here = wave_coeffs.shape[0]
    band_total = band_here * lax.axis_size("gy")
    atom_total = species_map.shape[0]
    atom_own = atom_total // lax.axis_size("gx")
    own_start = lax.axis_index("gx") * atom_own
    own_species = lax.dynamic_slice_in_dim(species_map, own_start, atom_own, 0)
    own_counts = lax.dynamic_slice_in_dim(proj_counts, own_start, atom_own, 0)
    current = wave_coeffs
    updated = wave_coeffs.astype(jnp.float32)
    for turn_index in range(ITERS):
        values = current.astype(jnp.float32)
        local_norm = jnp.sum(values * values, axis=1)
        local_kin = jnp.sum(kinetic[None, :] * values * values, axis=1)
        operand = current
        held_rows = lax.psum_scatter(
            lax.dot_general(
                projectors, operand, (((1,), (1,)), ((), ())), preferred_element_type=jnp.float32
            ),
            "gx",
            scatter_dimension=0,
            tiled=True,
        )
        raw_proj = held_rows.reshape(-1, PMAX, band_here)
        live_slots = live_table(own_counts, PMAX)
        masked = raw_proj * live_slots[:, :, None]
        local_density = (
            jnp.einsum(
                "apb,aqb->apq",
                masked * occupations[None, None, :],
                masked,
                precision=lax.Precision.HIGHEST,
            )
            / band_total
        )
        density = lax.psum(local_density, "gy")
        weighted = finish_onsite(masked, density, live_slots, own_species, onsite_base)
        weight_bf = weighted.reshape(-1, band_here).astype(jnp.bfloat16)
        nonlocal_part = lax.dot_general(
            lax.all_gather(weight_bf, "gx", axis=0, tiled=True),
            projectors,
            (((0,), (0,)), ((), ())),
            preferred_element_type=jnp.float32,
        )
        applied = kinetic[None, :] * values + nonlocal_part
        local_energy = jnp.sum(values * applied, axis=1)
        norm_sq, kin_sum, energy_sum = lax.psum((local_norm, local_kin, local_energy), "gx")
        eigen_value = energy_sum / norm_sq
        band_kinetic = kin_sum / norm_sq
        residual = applied - eigen_value[:, None] * values
        updated = values - step_length * teter_factor(kinetic, band_kinetic) * residual
        if turn_index + 1 < ITERS:
            current = updated.astype(jnp.bfloat16)
    return updated


def solution(mesh):
    placed = (P("gy", "gx"), P(None, "gx"), P(None, "gx"), P("gy"), P(), P(), P())
    return jax.shard_map(
        local, mesh=mesh, in_specs=placed, out_specs=P("gy", "gx"), check_vma=False
    )
```

profile of v0, /device:TPU:1, one launch (start us, length us, event | category | flops | bytes accessed | tf_op | source)
XLA Modules:
  0.0 461.2 jit_solution(17467189755516672734)
XLA Ops:
  6.5 0.0 copy-start.3
  6.5 0.0 copy-start
  6.5 0.0 copy-start.5
  6.5 0.0 copy-start.6
  6.5 0.0 copy-start.2
  6.5 0.0 copy-start.1
  6.6 0.0 copy-start.4
  6.6 0.0 reduce-scatter.5.cloned.1.call-start
  6.6 7.2 %fusion.45 = f32[1024,192]{1,0:T(8,128)} fusion(bf16[1024,4096]{1,0:T(8,128)(2,1)} %param.9, bf16[192,4096]{1,0:T(8,128)(2,1)} %param.8), kind=kOutput, calls=%fused_computation.72 | convolution fusion | flops 1610612736 | bytes 10747904 | tf_op jit(solution)/shard_map/dot_general | solution.py:70
  13.8 0.0 reduce-scatter.5.cloned.1.call-update
  13.9 0.0 reduce-scatter.7.cloned.1.call-start
  13.9 0.0 copy-done.5
  13.9 0.1 dynamic_slice.6
  14.0 0.0 copy-done.6
  14.0 0.1 dynamic_slice.7
  14.1 0.0 copy-done.2
  14.1 0.1 copy.25
  14.2 0.1 reshape.49
  14.3 0.1 dot_general.35
  14.3 0.0 copy-done.3
  14.3 0.0 copy-done.1
  14.3 0.1 fusion.17
  14.5 0.1 fusion.39
  14.5 0.2 fusion.21
  14.7 86.6 %reduce-scatter.5.cloned.1.call-done = f32[32,192]{1,0:T(8,128)} async-done(((f32[1024,192]{1,0:T(8,128)}), f32[32,192]{1,0:T(8,128)}) %reduce-scatter.5.cloned.1.call-update) | async-done | bytes 24592 | tf_op jit(solution)/shard_map/reduce_scatter | solution.py:69
  101.3 0.0 copy-done.4
  101.3 1.1 convolution_multiply_fusion.3
  102.4 23.1 %psum.58 = f32[4,8,8]{2,1,0:T(8,128)S(1)} all-reduce(f32[4,8,8]{2,1,0:T(8,128)S(1)} %convolution_multiply_fusion.3), channel_id=1, replica_groups=mesh['gx'=32,'gy'=8] {'gy'}, use_global_device_ids=true, to_apply=%region_6.0 | all-reduce | flops 256 | bytes 2048 | tf_op jit(solution)/shard_map/psum | solution.py:89
  125.4 1.0 fusion.16
  126.4 33.4 %all_gather.6 = bf16[1024,192]{1,0:T(8,128)(2,1)S(1)} all-gather(bf16[32,192]{1,0:T(8,128)(2,1)S(1)} %fusion.16), channel_id=1, replica_groups=mesh['gx'=32,'gy'=8] {'gx'}, dimensions={0}, use_global_device_ids=true | all-gather | bytes 405504 | tf_op jit(solution)/shard_map/all_gather | solution.py:93
  159.8 0.0 copy-done
  159.8 7.7 %fusion.4 = (f32[192]{0:T(256)S(1)}, f32[192]{0:T(256)S(1)}, f32[192]{0:T(256)S(1)}, f32[192,4096]{1,0:T(8,128)}) fusion(bf16[192,4096]{1,0:T(8,128)(2,1)S(1)} %copy-done, f32[4096]{0:T(1024)S(1)} %broadcast_multiply_fusion, bf16[1024,192]{1,0:T(8,128)(2,1)S(1)} %all_gather.6, bf16[1024,4096]{1,0:T(8,128)(2,1)} %param.9), kind=kOutput, calls=%fused_computation.20 | convolution fusion | flops 1617690112 | bytes 13519104 | tf_op jit(solution)/shard_map/dot_general | solution.py:92
  167.5 62.2 %all-reduce.1 = (f32[192]{0:T(256)S(1)}, f32[192]{0:T(256)S(1)}, f32[192]{0:T(256)S(1)}) all-reduce(f32[192]{0:T(256)S(1)} %get-tuple-element.10, f32[192]{0:T(256)S(1)} %get-tuple-element.9, f32[192]{0:T(256)S(1)} %get-tuple-element.8), channel_id=1, replica_groups=mesh['gx'=32,'gy'=8] {'gx'}, use_global_device_ids=true, to_apply=%region_8.0 | all-reduce | flops 576 | bytes 4608 | tf_op jit(solution)/shard_map/psum | solution.py:100
  229.7 3.7 fusion.12
  233.4 6.3 %convolution_bitcast_fusion = f32[1024,192]{0,1:T(8,128)S(1)} fusion(bf16[192,4096]{1,0:T(8,128)(2,1)S(1)} %fusion.12, bf16[1024,4096]{1,0:T(8,128)(2,1)} %param.9), kind=kOutput, calls=%fused_computation.29 | convolution fusion | flops 1610612736 | bytes 10747904 | tf_op jit(solution)/shard_map/dot_general | solution.py:70
  239.7 1.3 copy.30
  241.0 0.0 reduce-scatter.7.cloned.1.call-update
  241.0 80.0 %reduce-scatter.7.cloned.1.call-done = f32[32,192]{1,0:T(8,128)} async-done(((f32[1024,192]{1,0:T(8,128)}), f32[32,192]{1,0:T(8,128)}) %reduce-scatter.7.cloned.1.call-update) | async-done | bytes 24592 | tf_op jit(solution)/shard_map/reduce_scatter | solution.py:69
  321.0 1.1 convolution_multiply_fusion.2
  322.1 23.1 %psum.62 = f32[4,8,8]{2,1,0:T(8,128)S(1)} all-reduce(f32[4,8,8]{2,1,0:T(8,128)S(1)} %convolution_multiply_fusion.2), channel_id=1, replica_groups=mesh['gx'=32,'gy'=8] {'gy'}, use_global_device_ids=true, to_apply=%region_14.0 | all-reduce | flops 256 | bytes 2048 | tf_op jit(solution)/shard_map/psum | solution.py:89
  345.2 1.0 fusion.15
  346.2 33.5 %all_gather.7 = bf16[1024,192]{1,0:T(8,128)(2,1)S(1)} all-gather(bf16[32,192]{1,0:T(8,128)(2,1)S(1)} %fusion.15), channel_id=1, replica_groups=mesh['gx'=32,'gy'=8] {'gx'}, dimensions={0}, use_global_device_ids=true | all-gather | bytes 405504 | tf_op jit(solution)/shard_map/all_gather | solution.py:93
  379.8 7.7 %fusion.8 = (f32[192]{0:T(256)S(1)}, f32[192]{0:T(256)S(1)}, f32[192]{0:T(256)S(1)}, f32[192,4096]{1,0:T(8,128)}) fusion(bf16[192,4096]{1,0:T(8,128)(2,1)S(1)} %fusion.12, f32[4096]{0:T(1024)S(1)} %broadcast_multiply_fusion, bf16[1024,192]{1,0:T(8,128)(2,1)S(1)} %all_gather.7, bf16[1024,4096]{1,0:T(8,128)(2,1)} %param.9), kind=kOutput, calls=%fused_computation.24 | convolution fusion | flops 1617690112 | bytes 13519104 | tf_op jit(solution)/shard_map/dot_general | solution.py:92
  387.5 62.2 %all-reduce = (f32[192]{0:T(256)S(1)}, f32[192]{0:T(256)S(1)}, f32[192]{0:T(256)S(1)}) all-reduce(f32[192]{0:T(256)S(1)} %get-tuple-element.7, f32[192]{0:T(256)S(1)} %get-tuple-element.6, f32[192]{0:T(256)S(1)} %get-tuple-element.5), channel_id=1, replica_groups=mesh['gx'=32,'gy'=8] {'gx'}, use_global_device_ids=true, to_apply=%region_16.0 | all-reduce | flops 576 | bytes 4608 | tf_op jit(solution)/shard_map/psum | solution.py:100
  449.6 4.7 %convert_subtract_fusion = f32[192,4096]{1,0:T(8,128)} fusion(bf16[192,4096]{1,0:T(8,128)(2,1)S(1)} %fusion.12, f32[192,4096]{1,0:T(8,128)} %get-tuple-element.22, f32[192]{0:T(256)S(1)} %get-tuple-element.18, f32[192]{0:T(256)S(1)} %get-tuple-element.17, f32[4096]{0:T(1024)S(1)} %broadcast_multiply_fusion), kind=kLoop, calls=%fused_computation | loop fusion | flops 14155776 | bytes 7882240 | tf_op jit(solution)/shard_map/sub | solution.py:104
  (4 shorter events, 0.0 us)
Async XLA Ops:
  6.5 7.8 %copy-start.3 = (f32[3]{0:T(128)S(1)}, f32[3]{0:T(128)}, u32[]{:S(2)}) copy-start(f32[3]{0:T(128)} %constant.37.clone) | copy-start | bytes 40
  6.5 153.3 %copy-start = (bf16[192,4096]{1,0:T(8,128)(2,1)S(1)}, bf16[192,4096]{1,0:T(8,128)(2,1)}, u32[]{:S(2)}) copy-start(bf16[192,4096]{1,0:T(8,128)(2,1)} %param.8) | copy-start | bytes 4718596
  6.5 7.4 %copy-start.5 = (s32[128]{0:T(128)S(1)}, s32[128]{0:T(128)}, u32[]{:S(2)}) copy-start(s32[128]{0:T(128)} %param.12) | copy-start | bytes 1540
  6.5 7.5 %copy-start.6 = (s32[128]{0:T(128)S(1)}, s32[128]{0:T(128)}, u32[]{:S(2)}) copy-start(s32[128]{0:T(128)} %param.13) | copy-start | bytes 1540
  6.5 7.5 %copy-start.2 = (f32[4,8,8]{2,1,0:T(8,128)S(1)}, f32[4,8,8]{2,1,0:T(8,128)}, u32[]{:S(2)}) copy-start(f32[4,8,8]{2,1,0:T(8,128)} %param.14) | copy-start | bytes 3076
  6.5 7.8 %copy-start.1 = (s32[3,4096]{1,0:T(4,128)S(1)}, s32[3,4096]{1,0:T(4,128)}, u32[]{:S(2)}) copy-start(s32[3,4096]{1,0:T(4,128)} %param.10) | copy-start | bytes 147460
  6.6 94.7 %copy-start.4 = (f32[192]{0:T(256)S(1)}, f32[192]{0:T(256)}, u32[]{:S(2)}) copy-start(f32[192]{0:T(256)} %param.11) | copy-start | bytes 2308
  6.6 94.7 %reduce-scatter.5.cloned.1.call-start = ((), (), s32[]{:S(2)}) async-start(), calls=%async_computation.2 | async-start | bytes 1081344 | tf_op jit(solution)/shard_map/reduce_scatter | solution.py:69
  13.9 307.2 %reduce-scatter.7.cloned.1.call-start = ((), (), s32[]{:S(2)}) async-start(), calls=%async_computation.3 | async-start | bytes 1081344 | tf_op jit(solution)/shard_map/reduce_scatter | solution.py:69
Sparse Core Ops, SparseCore 0:
  14.0 87.2 reduce-scatter.4
  241.1 79.8 reduce-scatter.6
where the time goes:
time: 462 us; the launch traced here: 461 us
  blocking collectives  237 us (51%)
  waiting for transfers between devices  167 us (36%)
  matrix products  33.2 us (7%)
  between operations  13.5 us (3%)
  other arithmetic  8.61 us (2%)
    reduce_scatter x2, waiting for transfers between devices, local(): lax.psum_scatter(lax.dot_general(projectors, operand, (((1,), (1,)), ((),...  167 us
    psum x2, blocking collectives, local(): lax.psum((local_norm, local_kin, local_energy), 'gx')  124 us
    all_gather x2, blocking collectives, local(): lax.all_gather(weight_bf, 'gx', axis=0, tiled=True)  66.9 us
    psum x2, blocking collectives, local(): density = lax.psum(local_density, 'gy')  46.2 us
    dot_general x2, matrix products, local(): lax.dot_general(lax.all_gather(weight_bf, 'gx', axis=0, tiled=True), proj...  15.4 us
    dot_general x2, matrix products, local(): lax.dot_general(projectors, operand, (((1,), (1,)), ((), ())), preferred_...  13.5 us
  transfers between devices with their start and end apart: 2, of which 2 were waited for; matrix products, arithmetic and copies ran while one was open for 0% of the time, Pallas kernels for 0%

commit v1 on v0

v1 whole, which is shorter than its diff:
```python
import functools

import jax
import jax.numpy as jnp
from jax import lax
from jax.experimental import pallas as pl
from jax.experimental.pallas import tpu as pltpu
from jax.sharding import PartitionSpec as P

PMAX = 8
ITERS = 2
KINETIC_UNIT = 1.0 / 600.0
HUBBARD = 2.0
STEP = 0.5
MESH = pl.DeviceIdType.MESH
HIGH = lax.Precision.HIGHEST
F32, BF16 = jnp.float32, jnp.bfloat16

SIDE = 4
CHIPS = SIDE * SIDE
OWN = 32
HALF = CHIPS * OWN
PART = HALF // 2
LANES = 256
COLS = 1024
DEPTH = 512


def hops(step):
    return min(step, SIDE - step)


STEPS = sorted(
    ((dy, dx) for dy in range(SIDE) for dx in range(SIDE)), key=lambda s: -(hops(s[0]) + hops(s[1]))
)
BACK = [STEPS.index(((-dy) % SIDE, (-dx) % SIDE)) for dy, dx in STEPS]


def pieces(q):
    hi = q.astype(BF16).astype(F32)
    mid = (q - hi).astype(BF16).astype(F32)
    low = q - hi - mid
    return jnp.concatenate([hi, mid, low, jnp.zeros_like(q)], axis=0)


def whole(parts):
    return parts[0:8] + parts[8:16] + parts[16:24]


def columns_of(q, at, band_here):
    t = jnp.concatenate([q, jnp.zeros((120, 128), F32)], axis=0).T
    return jnp.concatenate([t[64:128, at(i) : at(i) + 1] for i in range(band_here // 64)], axis=0)


def kernel(
    z_count,
    band_total,
    wave,
    proj,
    miller_in,
    occ_in,
    species_in,
    counts_in,
    base_in,
    out,
    miller,
    occ,
    species,
    counts,
    base,
    p_v,
    cur,
    nl,
    hf,
    kin,
    norm_acc,
    kin_acc,
    cols,
    sib_send,
    sib_recv,
    send,
    recv,
    z_send,
    z_recv,
    w_all,
    w_t,
    small_sem,
    p_sem,
    cur_sem,
    sib_ssem,
    sib_rsem,
    ssem,
    rsem,
    z_ssem,
    z_rsem,
    w_ssem,
    w_rsem,
    ws_ssem,
    ws_rsem,
):
    gx, gy = lax.axis_index("gx"), lax.axis_index("gy")
    band_here = wave.shape[0]
    waves = wave.shape[1]
    core = lax.rem(gx, 2)
    chip = gx // 2
    cy, cx = chip // SIDE, lax.rem(chip, SIDE)

    def owner(j, which):
        dy, dx = STEPS[j]
        return (lax.rem(cy + dy, SIDE) * SIDE + lax.rem(cx + dx, SIDE)) * 2 + which

    sibling = (chip * 2 + 1 - core, gy)

    wave_copy = pltpu.make_async_copy(wave, cur.at[pl.ds(0, band_here)], cur_sem)
    wave_copy.start()
    small = [
        pltpu.make_async_copy(source, held, small_sem.at[i])
        for i, (source, held) in enumerate(
            [
                (miller_in, miller),
                (species_in, species),
                (counts_in, counts),
                (base_in, base),
                (occ_in, occ),
            ]
        )
    ]
    for copy in small:
        copy.start()

    def load(part):
        which = 1 - core if part < 2 else core
        for i in range(CHIPS // 2):
            j = (part % 2) * (CHIPS // 2) + i
            rows = pl.ds(pl.multiple_of(owner(j, which) * OWN, OWN), OWN)
            pltpu.make_async_copy(
                proj.at[rows], p_v.at[pl.ds(part * PART + i * OWN, OWN)], p_sem.at[part]
            ).start()

    load(0)
    load(1)

    barrier = pltpu.get_barrier_semaphore()
    for j in range(CHIPS - 1):
        pl.semaphore_signal(barrier, inc=1, device_id=(owner(j, core), gy), device_id_type=MESH)
    for d in range(1, z_count):
        pl.semaphore_signal(
            barrier, inc=1, device_id=(gx, lax.rem(gy + d, z_count)), device_id_type=MESH
        )
    pl.semaphore_signal(barrier, inc=1, device_id=sibling, device_id_type=MESH)

    for copy in small:
        copy.wait()
    mi = miller[...].astype(F32)
    kin[...] = jnp.broadcast_to(
        (1.5 * mi[0:1] * mi[0:1] + 1.0 * mi[1:2] * mi[1:2] + 0.5 * mi[2:3] * mi[2:3]) * KINETIC_UNIT,
        kin.shape,
    )
    atoms_own = OWN // PMAX
    first = gx * atoms_own
    row_atom = lax.broadcasted_iota(jnp.int32, (OWN, band_here), 0) // PMAX
    row_slot = lax.broadcasted_iota(jnp.int32, (OWN, band_here), 0) % PMAX
    lane_atom = lax.broadcasted_iota(jnp.int32, (PMAX, OWN), 1) // PMAX
    row_count = jnp.zeros((OWN, band_here), jnp.int32)
    lane_kind = jnp.zeros((PMAX, OWN), jnp.int32)
    for a in range(atoms_own):
        row_count = jnp.where(row_atom == a, counts[first + a], row_count)
        lane_kind = jnp.where(lane_atom == a, species[first + a], lane_kind)
    live = (row_slot < row_count).astype(F32)
    base_own = jnp.zeros((PMAX, OWN), F32)
    for s in range(base.shape[0]):
        symmetric = 0.5 * (base[s] + base[s].T)
        base_own = jnp.where(
            lane_kind == s, jnp.concatenate([symmetric] * atoms_own, axis=1), base_own
        )
    same_atom = (
        lax.broadcasted_iota(jnp.int32, (OWN, OWN), 0) // PMAX
        == lax.broadcasted_iota(jnp.int32, (OWN, OWN), 1) // PMAX
    )
    lane = lax.broadcasted_iota(jnp.int32, (64, 128), 1)

    def add_norms(values, kin_tile):
        width = values.shape[1]
        sq = values * values
        ksq = kin_tile * sq
        n_part, k_part = sq[:, 0:128], ksq[:, 0:128]
        for i in range(1, width // 128):
            n_part = n_part + sq[:, i * 128 : (i + 1) * 128]
            k_part = k_part + ksq[:, i * 128 : (i + 1) * 128]
        norm_acc[...] += n_part
        kin_acc[...] += k_part

    def zero_norms():
        norm_acc[...] = jnp.zeros_like(norm_acc)
        kin_acc[...] = jnp.zeros_like(kin_acc)

    def packed_norms():
        stack = jnp.zeros((64, 128), F32)
        for i in range(band_here // 64):
            rows = slice(64 * i, 64 * i + 64)
            stack = jnp.where(lane == 2 * i, norm_acc[rows].sum(axis=1, keepdims=True), stack)
            stack = jnp.where(lane == 2 * i + 1, kin_acc[rows].sum(axis=1, keepdims=True), stack)
        return jnp.concatenate([jnp.zeros((64, 128), F32), stack], axis=0).T[0:8]

    cur[pl.ds(band_here, LANES - band_here)] = jnp.zeros((LANES - band_here, waves), BF16)
    wave_copy.wait()
    zero_norms()

    def first_norms(t, _):
        tile = pl.ds(pl.multiple_of(t * DEPTH, DEPTH), DEPTH)
        add_norms(cur[pl.ds(0, band_here), tile].astype(F32), kin[0:1, tile])
        return 0

    lax.fori_loop(0, waves // DEPTH, first_norms, 0)

    for it in range(ITERS):
        last = it == ITERS - 1

        def intersect(part):
            return lax.dot_general(
                p_v[pl.ds(part * PART, PART)],
                cur[...],
                (((1,), (1,)), ((), ())),
                preferred_element_type=F32,
            )

        def load_wait(part):
            if it == 0:
                rows = p_v.at[pl.ds(part * PART, PART)]
                pltpu.make_async_copy(rows, rows, p_sem.at[part]).wait()
                if part < 2:
                    load(part + 2)

        own_norms = packed_norms()
        sib_copies = []
        for part in range(2):
            load_wait(part)
            sums = intersect(part)
            rows = pl.ds(part * PART, PART)
            sib_send[it, rows, 0:128] = sums[:, 0:128].astype(BF16)
            sib_send[it, rows, 128:256] = sums[:, 128:256].astype(BF16)
            if part == 0:
                sib_send[it, pl.ds(0, OWN), 128:256] = (sums[0:OWN, 128:256] + pieces(own_norms)).astype(BF16)
            if it == 0 and part == 0:
                pl.semaphore_wait(barrier, CHIPS - 1 + z_count - 1 + 1)
            copy = pltpu.make_async_remote_copy(
                sib_send.at[it, rows],
                sib_recv.at[it, rows],
                sib_ssem.at[it, part],
                sib_rsem.at[it, part],
                device_id=sibling,
                device_id_type=MESH,
            )
            copy.start()
            sib_copies.append(copy)
        sends = []
        for part in range(2):
            load_wait(2 + part)
            sums = intersect(2 + part)
            rows = pl.ds(part * PART, PART)
            sib_copies[part].wait_recv()
            both = sums + sib_recv[it, rows].astype(F32)
            if part == 0:
                pair_norms = own_norms + whole(sib_recv[it, pl.ds(0, OWN), 128:256].astype(F32))
                pair_pieces = jnp.where(
                    lax.broadcasted_iota(jnp.int32, (OWN, 128), 1) >= 64, pieces(pair_norms), 0.0
                )
            tail = jnp.where(
                lax.broadcasted_iota(jnp.int32, (PART, 128), 1) < 64, both[:, 128:256], 0.0
            ) + jnp.concatenate([pair_pieces] * (PART // OWN), axis=0)
            send[it, rows, 0:128] = both[:, 0:128].astype(BF16)
            send[it, rows, 128:256] = tail.astype(BF16)
            for i in range(CHIPS // 2):
                j = part * (CHIPS // 2) + i
                if j < CHIPS - 1:
                    pltpu.make_async_remote_copy(
                        send.at[it, pl.ds(j * OWN, OWN)],
                        recv.at[it, pl.ds(j * OWN, OWN)],
                        ssem.at[it],
                        rsem.at[it],
                        device_id=(owner(j, core), gy),
                        device_id_type=MESH,
                    ).start()
            if part == 1:
                own_head = both[PART - OWN : PART, 0:128]
                own_tail = both[PART - OWN : PART, 128:256]
        pltpu.make_async_copy(recv.at[it], recv.at[it], rsem.at[it]).wait()
        head = own_head
        tail = jnp.where(
            lax.broadcasted_iota(jnp.int32, (OWN, 128), 1) >= 64, pieces(pair_norms), own_tail
        )
        for j in range(CHIPS - 1):
            rows = pl.ds(j * OWN, OWN)
            head = head + recv[it, rows, 0:128].astype(F32)
            tail = tail + recv[it, rows, 128:256].astype(F32)
        masked = jnp.concatenate([head, tail[:, 0 : band_here - 128]], axis=1) * live

        dense = lax.dot_general(
            masked,
            masked * occ[...],
            (((1,), (1,)), ((), ())),
            preferred_element_type=F32,
            precision=HIGH,
        )
        dense = jnp.where(same_atom, dense, 0.0)
        mine = dense[0:8] + dense[8:16] + dense[16:24] + dense[24:32]
        z_send[it, :, 0:OWN] = mine
        for d in range(1, z_count):
            pltpu.make_async_remote_copy(
                z_send.at[it],
                z_recv.at[it, d - 1],
                z_ssem.at[it],
                z_rsem.at[it],
                device_id=(gx, lax.rem(gy + d, z_count)),
                device_id_type=MESH,
            ).start()

        total = whole(tail)
        norm_col = columns_of(total, lambda i: 2 * i, band_here)
        kin_col = columns_of(total, lambda i: 2 * i + 1, band_here)
        inverse = norm_col / kin_col

        cols[0] = jnp.broadcast_to(inverse, (band_here, 128))

        def factors(t, _):
            tile = pl.ds(pl.multiple_of(t * 128, 128), 128)
            x = kin[0:1, tile] * cols[0]
            n = 27.0 + x * (18.0 + x * (12.0 + 8.0 * x))
            x2 = x * x
            hf[:, tile] = STEP * (n / (n + 16.0 * (x2 * x2)))
            return 0

        lax.fori_loop(0, waves // 128, factors, 0)

        pltpu.make_async_copy(z_recv.at[it], z_recv.at[it], z_rsem.at[it]).wait()
        for d in range(z_count - 1):
            mine = mine + z_recv[it, d, :, 0:OWN]
        onsite = base_own + HUBBARD * (mine / band_total)
        blocks = jnp.where(same_atom, jnp.concatenate([onsite] * atoms_own, axis=0), 0.0)
        weighted = (
            lax.dot_general(
                blocks,
                masked,
                (((0,), (0,)), ((), ())),
                preferred_element_type=F32,
                precision=HIGH,
            )
            * live
        )
        rounded = weighted.astype(BF16).astype(F32)
        energy = jnp.sum(rounded * masked, axis=0, keepdims=True)
        e_head, e_tail = energy[:, 0:128], energy[:, 128:band_here]
        e_tail = jnp.concatenate([e_tail, jnp.zeros((1, 256 - band_here), F32)], axis=1)
        row = lax.broadcasted_iota(jnp.int32, (8, 128), 0)
        e_rows = jnp.where(row == 0, pltpu.roll(jnp.broadcast_to(e_head, (8, 128)), 64, 1), 0.0)
        e_rows = jnp.where(row == 1, jnp.broadcast_to(e_head, (8, 128)), e_rows)
        e_rows = jnp.where(row == 2, pltpu.roll(jnp.broadcast_to(e_tail, (8, 128)), 64, 1), e_rows)
        w_tail = jnp.concatenate(
            [rounded[:, 128:band_here], jnp.zeros((OWN, 256 - band_here), F32)], axis=1
        )
        w_tail = jnp.where(
            lax.broadcasted_iota(jnp.int32, (OWN, 128), 1) >= 64, pieces(e_rows), w_tail
        )
        own_rows = pl.ds(2 * HALF - OWN, OWN)
        w_all[it, own_rows, 0:128] = rounded[:, 0:128].astype(BF16)
        w_all[it, own_rows, 128:256] = w_tail.astype(BF16)
        for j in range(CHIPS - 1):
            pltpu.make_async_remote_copy(
                w_all.at[it, own_rows],
                w_all.at[it, pl.ds(HALF + BACK[j] * OWN, OWN)],
                w_ssem.at[it],
                w_rsem.at[it, BACK[j] // (CHIPS // 2)],
                device_id=(owner(j, core), gy),
                device_id_type=MESH,
            ).start()

        def arrived(part):
            come = w_all.at[it, pl.ds(HALF + part * PART, PART if part == 0 else PART - OWN)]
            pltpu.make_async_copy(come, come, w_rsem.at[it, part]).wait()

        def forward(part):
            copy = pltpu.make_async_remote_copy(
                w_all.at[it, pl.ds(HALF + part * PART, PART)],
                w_all.at[it, pl.ds(part * PART, PART)],
                ws_ssem.at[it, part],
                ws_rsem.at[it, part],
                device_id=sibling,
                device_id_type=MESH,
            )
            copy.start()
            return copy

        def turn(quarter):
            w_t[:, quarter * PART : (quarter + 1) * PART] = w_all[
                it, pl.ds(quarter * PART, PART), 0:band_here
            ].T

        def product(low, high, tile):
            return jnp.dot(
                w_t[:, low * PART : high * PART],
                p_v[pl.ds(low * PART, (high - low) * PART), tile],
                preferred_element_type=F32,
            )

        arrived(1)
        near = forward(1)
        turn(3)

        def own_near(t, _):
            tile = pl.ds(pl.multiple_of(t * COLS, COLS), COLS)
            nl[:, tile] = product(3, 4, tile)
            return 0

        lax.fori_loop(0, waves // COLS, own_near, 0, unroll=True)
        arrived(0)
        far = forward(0)
        turn(2)
        near.wait_recv()
        turn(1)

        def middle(t, _):
            tile = pl.ds(pl.multiple_of(t * COLS, COLS), COLS)
            nl[:, tile] += product(1, 3, tile)
            return 0

        lax.fori_loop(0, waves // COLS, middle, 0, unroll=True)
        far.wait_recv()
        turn(0)
        parts = w_all[it, pl.ds(0, OWN), 128:256].astype(F32)
        for i in range(1, 2 * CHIPS):
            parts = parts + w_all[it, pl.ds(i * OWN, OWN), 128:256].astype(F32)
        energy_col = columns_of(whole(parts), lambda i: i, band_here)
        eigen = (kin_col + energy_col) / norm_col
        cols[1] = jnp.broadcast_to(eigen, (band_here, 128))
        zero_norms()

        def update(t, _):
            tile = pl.ds(pl.multiple_of(t * COLS, COLS), COLS)
            nonlocal_part = nl[:, tile] + product(0, 1, tile)
            v = cur[pl.ds(0, band_here), tile].astype(F32)
            shift = kin[0:1, tile] - jnp.concatenate([cols[1]] * (COLS // 128), axis=1)
            u = v - hf[:, tile] * (nonlocal_part + shift * v)
            if last:
                out[:, tile] = u
            else:
                new = u.astype(BF16)
                cur[pl.ds(0, band_here), tile] = new
                add_norms(new.astype(F32), kin[0:1, tile])
            return 0

        lax.fori_loop(0, waves // COLS, update, 0, unroll=True)

        for part in range(2):
            sib_copies[part].wait_send()
        gone = send.at[it, pl.ds(0, HALF - OWN)]
        pltpu.make_async_copy(gone, gone, ssem.at[it]).wait()
        pltpu.make_async_copy(z_recv.at[it], z_recv.at[it], z_ssem.at[it]).wait()
        gone = w_all.at[it, pl.ds(HALF, HALF - OWN)]
        pltpu.make_async_copy(gone, gone, w_ssem.at[it]).wait()
        near.wait_send()
        far.wait_send()


def local(wave, proj, miller, occ, species, counts, base):
    bands, waves = wave.shape
    slots = proj.shape[0]
    z_count = lax.axis_size("gy")
    hbm = pl.BlockSpec(memory_space=pltpu.HBM)
    dma = pltpu.SemaphoreType.DMA
    return pl.pallas_call(
        functools.partial(kernel, z_count, bands * z_count),
        out_shape=jax.ShapeDtypeStruct((bands, waves), F32),
        in_specs=[hbm] * 7,
        out_specs=pl.BlockSpec(memory_space=pltpu.VMEM),
        scratch_shapes=[
            pltpu.VMEM(miller.shape, jnp.int32),
            pltpu.VMEM((1, bands), F32),
            pltpu.SMEM(species.shape, jnp.int32),
            pltpu.SMEM(counts.shape, jnp.int32),
            pltpu.VMEM(base.shape, F32),
            pltpu.VMEM((slots, waves), BF16),
            pltpu.VMEM((LANES, waves), BF16),
            pltpu.VMEM((bands, waves), F32),
            pltpu.VMEM((bands, waves), F32),
            pltpu.VMEM((8, waves), F32),
            pltpu.VMEM((bands, 128), F32),
            pltpu.VMEM((bands, 128), F32),
            pltpu.VMEM((2, bands, 128), F32),
            pltpu.VMEM((ITERS, HALF, LANES), BF16),
            pltpu.VMEM((ITERS, HALF, LANES), BF16),
            pltpu.VMEM((ITERS, HALF, LANES), BF16),
            pltpu.VMEM((ITERS, HALF - OWN, LANES), BF16),
            pltpu.VMEM((ITERS, 8, 128), F32),
            pltpu.VMEM((ITERS, z_count - 1, 8, 128), F32),
            pltpu.VMEM((ITERS, 2 * HALF, LANES), BF16),
            pltpu.VMEM((bands, 2 * HALF), BF16),
            dma((5,)),
            dma((4,)),
            dma,
            dma((ITERS, 2)),
            dma((ITERS, 2)),
            dma((ITERS,)),
            dma((ITERS,)),
            dma((ITERS,)),
            dma((ITERS,)),
            dma((ITERS,)),
            dma((ITERS, 2)),
            dma((ITERS, 2)),
            dma((ITERS, 2)),
        ],
        compiler_params=pltpu.CompilerParams(
            collective_id=1, has_side_effects=True, vmem_limit_bytes=36 * 2**20
        ),
        name="residual_updates",
    )(*[
        pltpu.with_memory_space_constraint(a, pltpu.HBM)
        for a in (wave, proj, miller, occ[None, :], species, counts, base)
    ])


def solution(mesh):
    placed = (P("gy", "gx"), P(None, "gx"), P(None, "gx"), P("gy"), P(), P(), P())
    return jax.shard_map(
        local, mesh=mesh, in_specs=placed, out_specs=P("gy", "gx"), check_vma=False
    )
```

time: 462 us -> 60.1 us (0.13)
  blocking collectives: 237 us -> 0 us
  waiting for transfers between devices: 167 us -> 0 us
  Pallas kernels: 0 us -> 58.4 us
  matrix products: 33.2 us -> 0 us
  between operations: 13.5 us -> 0.01 us
  other arithmetic: 8.61 us -> 0 us
    psum x4 -> x0, blocking collectives: 171 us -> none  [the longest x2 124 us: local(): lax.psum((local_norm, local_kin, local_energy), 'gx')]
    reduce_scatter x2 -> x0, waiting for transfers between devices: 167 us -> none  [local(): lax.psum_scatter(lax.dot_general(projectors, operand, (((1,), (1,)), ((),...]
    all_gather x2 -> x0, blocking collectives: 66.9 us -> none  [local(): lax.all_gather(weight_bf, 'gx', axis=0, tiled=True)]
    pallas_call x0 -> x1, Pallas kernels: none -> 58.4 us  [local(): pl.pallas_call(functools.partial(kernel, z_count, bands * z_count), out_s...]
    dot_general x9 -> x0, matrix products: 33.2 us -> none  [the longest x2 15.4 us: local(): lax.dot_general(lax.all_gather(weight_bf, 'gx', axis=0, tiled=True), proj...]
    sub x1 -> x0, other arithmetic: 4.69 us -> none  [local(): values - step_length * teter_factor(kinetic, band_kinetic) * residual]
  transfers between devices with their start and end apart: 2 -> 0, of which waited for: 2 -> 0; matrix products, arithmetic and copies ran while one was open for 0% -> 0% of each run, Pallas kernels for 0% -> 0%
where the time goes in v1:
time: 60.1 us
  Pallas kernels  58.4 us (97%)
  local copies, waits for them, and re-layouts  1.67 us (3%)
    pallas_call x1, Pallas kernels, local(): pl.pallas_call(functools.partial(kernel, z_count, bands * z_count), out_s...  58.4 us
    unnamed x1, local copies, waits for them, and re-layouts  1.67 us

profile of v1, /device:TPU:1, one launch (start us, length us, event | category | flops | bytes accessed | tf_op | source)
XLA Modules:
  0.0 60.1 jit_solution(12323219124222268578)
XLA Ops:
  0.0 58.4 %residual_updates.1 = f32[192,4096]{1,0:T(8,128)S(1)} custom-call(bf16[192,4096]{1,0:T(8,128)(2,1)} %wave.1, bf16[1024,4096]{1,0:T(8,128)(2,1)} %proj.1, s32[3,4096]{1,0:T(4,128)} %miller_in.1, f32[1,192]{1,0:T(1,128)} %bitcast.1, s32[128]{0:T(128)} %species_in.1, s32[128]{0:T(128)} %counts_in.1, f32[4,8,8]{2,1,0:T(8,128)} %base_in.1), custom_call_target="tpu_custom_call" | custom-call | tf_op jit(solution)/shard_map/residual_updates/pallas_call | solution.py:470
  58.4 1.7 %copy.9 = f32[192,4096]{1,0:T(8,128)} copy(f32[192,4096]{1,0:T(8,128)S(1)} %residual_updates.1) | data formatting | bytes 6291456
